TPU v7x, 128 devices: a whole 4x4x4 slice. The times are simulated.
128 devices in a mesh: row: 16 (over y, x), col: 8 (over z, core).
Axes of the slice: x: 4, y: 4, z: 4, core: 2. Of those that a mesh axis runs over, the one named last changes fastest.
Arguments:
- upper_block: float32 [2, 1024, 1024], P(None, 'row', 'col'), may hold values from -0.25 to 0.25
- block_inverse: float32 [2, 1024, 64], P(None, 'row'), may hold values from -0.375 to 0.375
- panel_rhs: float32 [2, 32, 1024], P(None, None, 'row'), may hold values from -6 to 6
- upper_trail: float32 [2, 1024, 131072], P(None, 'row', 'col'), may hold values from -0.125 to 0.125
- trail_rhs: float32 [2, 32, 131072], P(None, None, ('col', 'row')), may hold values from -6 to 6
- currents: float32 [2, 1024], P(None, 'row'), may hold values from -4 to 4
- owner: int32 [1024], P('row'), may hold values from 0 to 511
Outputs:
- panel_adjoint: float32 [2, 32, 1024], P(None, None, 'row')
- trail_updated: float32 [2, 32, 131072], P(None, None, ('col', 'row'))
- patch_gradient: float32 [512], P(('row', 'col'))
Inputs may be any that keep to these rules, and one draw needn't show every extreme that they name: owner names a surface patch for each panel unknown.
All inputs are finite; a program needn't handle non-finite values.
Results may differ from a plain program's by a relative error of at most 0.0003.
Values sent between devices are 32-bit elements; how exact they have to be, the bound alone decides.
A program may use at most 64 MiB of HBM per device.

v0:
```python
import jax
import jax.numpy as jnp
from jax import lax
from jax.sharding import Mesh
from jax.sharding import PartitionSpec as P

PATCH_DEV = 4
ROW = ("row_0", "row_1")
ROW_COL = ("row_0", "row_1", "col")
COL_ROW = ("col", "row_0", "row_1")
highest = lax.Precision.HIGHEST


def rows_first(arrays, axis, dims):
    turned = [jnp.moveaxis(a, dim, 0) for a, dim in zip(arrays, dims)]
    widths = [t[0].size for t in turned]
    both = jnp.concatenate([t.reshape(-1, w) for t, w in zip(turned, widths)], axis=1)
    filled = lax.all_gather(both, axis, axis=0, tiled=True)
    pieces = jnp.split(filled, [sum(widths[:k]) for k in range(1, len(widths))], axis=1)
    return tuple(
        (
            jnp.moveaxis(b.reshape(-1, *t.shape[1:]), 0, dim)
            for b, t, dim in zip(pieces, turned, dims)
        )
    )


def sum_by_axis(value, axes, dim):
    if not axes:
        return value
    nearer = lax.psum_scatter(value, axes[0], scatter_dimension=dim, tiled=True)
    return sum_by_axis(nearer, axes[1:], dim)


def product_high(first, second):
    return jnp.dot(first, second, precision=highest, preferred_element_type=jnp.float32)


def conj_product(left, right):
    real_part = product_high(left[0], right[0]) + product_high(left[1], right[1])
    imag_part = product_high(left[1], right[0]) - product_high(left[0], right[1])
    return jnp.stack([real_part, imag_part])


def sweep(upper, inverses, rhs, width):
    count = rhs.shape[2] // width
    held_start = jnp.zeros(rhs.shape, jnp.float32)
    solved_start = jnp.zeros(rhs.shape, jnp.float32)

    def advance(index, carry):
        held, solved = carry
        start = (jnp.asarray(index) * width).astype(jnp.int32)
        local = lax.dynamic_slice_in_dim(held, start, width, 2)
        residual = lax.dynamic_slice_in_dim(rhs, start, width, 2) - local
        inverse = lax.dynamic_slice_in_dim(inverses, start, width, 1)
        value = conj_product(residual, inverse)
        rows_here = lax.dynamic_slice_in_dim(upper, start, width, 1)
        held = held + conj_product(value, rows_here)
        solved = lax.dynamic_update_slice_in_dim(solved, value, start, 2)
        return (held, solved)

    return lax.fori_loop(0, count, advance, (held_start, solved_start))[1]


def on_device(upper_block, block_inverse, panel_rhs, upper_trail, trail_rhs, currents, owner):
    rows_count = lax.axis_size(ROW)
    cols_count = lax.axis_size("col")
    row_index = lax.axis_index(ROW)
    col_index = lax.axis_index("col")
    width = block_inverse.shape[1]
    whole_rows, inverses, rhs_all = rows_first(
        (upper_block, block_inverse, panel_rhs), ROW, (1, 1, 2)
    )
    whole = lax.all_gather(whole_rows, "col", axis=2, tiled=True)
    solved_all = sweep(whole, inverses, rhs_all, width)
    solved = lax.dynamic_slice_in_dim(solved_all, row_index * width, width, 2)
    term = conj_product(solved, upper_trail)
    reduced = sum_by_axis(term, ROW, 2)
    updated = trail_rhs - reduced
    share = width // cols_count
    start = col_index * share
    mine = lax.dynamic_slice_in_dim(solved, start, share, 2)
    total = jnp.sum(mine, axis=1)
    current_part = lax.dynamic_slice_in_dim(currents, start, share, 1)
    owner_part = lax.dynamic_slice_in_dim(owner, start, share, 0)
    partial_value = current_part[0] * total[0] - current_part[1] * total[1]
    patch_count = PATCH_DEV * rows_count * cols_count
    patch_ids = lax.broadcasted_iota(jnp.int32, (share, patch_count), 1)
    selector = (owner_part[:, None] == patch_ids).astype(jnp.float32)
    spread = product_high(partial_value[None, :], selector)[0]
    gradient = lax.psum_scatter(spread, ROW_COL, scatter_dimension=0, tiled=True)
    return (solved, updated, gradient)


def solution(mesh):
    split = Mesh(mesh.devices.reshape(4, 4, mesh.shape["col"]), ("row_0", "row_1", "col"))
    return jax.shard_map(
        on_device,
        mesh=split,
        in_specs=(
            P(None, ROW, "col"),
            P(None, ROW, None),
            P(None, None, ROW),
            P(None, ROW, "col"),
            P(None, None, COL_ROW),
            P(None, ROW),
            P(ROW),
        ),
        out_specs=(P(None, None, ROW), P(None, None, COL_ROW), P(ROW_COL)),
        check_vma=False,
    )
```

profile of v0, /device:TPU:1, one launch (start us, length us, event | category | flops | bytes accessed | tf_op | source)
XLA Modules:
  0.0 364.6 jit_solution(3339413474390331940)
XLA Ops:
  9.8 48.1 %all-gather.3.cloned.1.call-done = f32[1024,448]{1,0:T(8,128)} async-done(((f32[64,448]{1,0:T(8,128)}), f32[1024,448]{1,0:T(8,128)}) %all-gather.3.cloned.1.call-update) | async-done | bytes 1835024 | tf_op jit(solution)/shard_map/all_gather | solution.py:18
  57.9 1.4 split.14
  59.3 1.3 copy.31
  61.2 50.3 %all-gather.5.cloned.1.call-done = f32[2,1024,1024]{1,2,0:T(8,128)} async-done(((f32[2,1024,128]{1,2,0:T(8,128)}), f32[2,1024,1024]{1,2,0:T(8,128)}) %all-gather.5.cloned.1.call-update) | async-done | bytes 8388624 | tf_op jit(solution)/shard_map/all_gather | solution.py:74
  111.4 8.7 %copy.33 = f32[2,1024,1024]{2,1,0:T(8,128)} copy(f32[2,1024,1024]{1,2,0:T(8,128)} %all-gather.5.cloned.1.call-done) | data formatting | bytes 16777216
  120.1 106.3 %while.16 = (s32[]{:T(128)}, f32[2,32,1024]{2,1,0:T(8,128)S(1)}, f32[2,32,1024]{2,1,0:T(8,128)S(1)}, f32[2,32,1024]{2,1,0:T(8,128)S(1)}, f32[2,1024,64]{1,2,0:T(...) while((s32[]{:T(128)}, f32[2,32,1024]{2,1,0:T(8,128)S(1)}, ...), condition=%wide.region_1.0_spmd.clone, body=%wide.region_0.0_spmd.clone.sunk | while | flops 107294728 | bytes 3555570 | solution.py:62
  122.5 1.2 fusion.60
  129.0 1.2 fusion.60
  142.3 1.2 fusion.60
  149.1 1.2 fusion.60
  162.4 1.2 fusion.60
  168.9 1.2 fusion.60
  175.7 1.2 fusion.60
  182.2 1.2 fusion.60
  189.0 1.2 fusion.60
  202.3 1.2 fusion.60
  226.4 4.0 %fusion.20 = f32[32,16384]{1,0:T(8,128)S(1)} fusion(f32[2,64,16384]{2,1,0:T(8,128)} %param.12, f32[2,32,1024]{2,1,0:T(8,128)S(1)} %get-tuple-element.112, s32[]{:T(128)S(6)} %select_n.23), kind=kOutput, calls=%fused_computation.37 | convolution fusion | flops 402653184 | bytes 6307844 | tf_op jit(solution)/shard_map/dot_general | solution.py:36
  230.5 4.0 %fusion.18 = f32[32,16384]{1,0:T(8,128)S(1)} fusion(f32[2,64,16384]{2,1,0:T(8,128)} %param.12, f32[2,32,1024]{2,1,0:T(8,128)S(1)} %get-tuple-element.112, s32[]{:T(128)S(6)} %add.84, s32[]{:T(128)S(6)} %select_n.23), kind=kOutput, calls=%fused_computation.35 | convolution fusion | flops 402653184 | bytes 6307848 | tf_op jit(solution)/shard_map/dot_general | solution.py:36
  234.5 3.9 %fusion.14 = f32[1,32,16384]{2,1,0:T(8,128)S(1)} fusion(f32[32,16384]{1,0:T(8,128)S(1)} %fusion.18, f32[2,64,16384]{2,1,0:T(8,128)} %param.12, f32[2,32,1024]{2,1,0:T(8,128)S(1)} %get-tuple-element.112, s32[]{:T(128)S(6)} %select_n.23), kind=kOutput, calls=%fused_computation.29 | convolution fusion | flops 403177472 | bytes 8404996 | tf_op jit(solution)/shard_map/dot_general | solution.py:36
  238.5 2.2 fusion.15
  240.7 2.2 pad_maximum_fusion.1
  243.0 46.6 %reduce-scatter.3.cloned.1.call-done = f32[2,32,4096]{2,1,0:T(8,128)} async-done(((f32[2,32,16384]{2,1,0:T(8,128)}), f32[2,32,4096]{2,1,0:T(8,128)}) %reduce-scatter.3.cloned.1.call-update) | async-done | bytes 1048592 | tf_op jit(solution)/shard_map/reduce_scatter | solution.py:31
  290.1 65.0 %all-reduce = f32[512]{0:T(512)S(1)} all-reduce(f32[512]{0:T(512)S(1)} %bitcast.133), channel_id=4, replica_groups=mesh['row_0'=4,'row_1'=4,'col'=8] {'row_0','row_1','col'}, use_global_device_ids=true, to_apply=%region_5.0.clone | all-reduce | flops 512 | bytes 4096
  356.4 1.7 sub.32
  (239 shorter events, 96.9 us)
Async XLA Ops:
  7.2 1.9 copy-start
  7.2 50.8 %all-gather.3.cloned.1.call-start = ((), (), s32[]{:S(2)}) async-start(), calls=%async_computation.2 | async-start | bytes 2228224 | tf_op jit(solution)/shard_map/all_gather | solution.py:18
  9.8 101.7 %all-gather.5.cloned.1.call-start = ((), (), s32[]{:S(2)}) async-start(), calls=%async_computation.3 | async-start | bytes 9437184 | tf_op jit(solution)/shard_map/all_gather | solution.py:74
  57.9 2.8 slice-start.2
  57.9 3.0 slice-start.3
  60.7 228.9 %reduce-scatter.3.cloned.1.call-start = ((), (), s32[]{:S(2)}) async-start(), calls=%async_computation.4 | async-start | bytes 5242880 | tf_op jit(solution)/shard_map/reduce_scatter | solution.py:31
  226.4 12.1 %slice-start = ((s8[8388608]{0:T(1024)(128)(4,1)}), s8[4194304]{0:T(1024)(128)(4,1)S(1)}, s32[]{:S(2)}) async-start(s8[8388608]{0:T(1024)(128)(4,1)} %bitcast.124), calls=%async_computation.6 | async-start | bytes 8388608
  230.5 8.0 %slice-start.1 = ((s8[8388608]{0:T(1024)(128)(4,1)}), s8[4194304]{0:T(1024)(128)(4,1)S(1)}, s32[]{:S(2)}) async-start(s8[8388608]{0:T(1024)(128)(4,1)} %bitcast.124), calls=%async_computation.7 | async-start | bytes 8388608
  242.9 46.7 %copy-start.3 = (s32[64]{0:T(128)S(1)}, s32[64]{0:T(128)}, u32[]{:S(2)}) copy-start(s32[64]{0:T(128)} %param.15) | copy-start | bytes 772
  242.9 46.8 %copy-start.2 = (f32[2,64]{1,0:T(2,128)S(1)}, f32[2,64]{1,0:T(2,128)}, u32[]{:S(2)}) copy-start(f32[2,64]{1,0:T(2,128)} %param.14) | copy-start | bytes 1540
  242.9 113.4 %copy-start.1 = (f32[2,32,1024]{2,1,0:T(8,128)S(1)}, f32[2,32,1024]{2,1,0:T(8,128)}, u32[]{:S(2)}) copy-start(f32[2,32,1024]{2,1,0:T(8,128)} %param.13) | copy-start | bytes 786436
  243.0 113.4 %reduce-scatter.5.cloned.1.call-start = ((), (), s32[]{:S(2)}) async-start(), calls=%async_computation.5 | async-start | bytes 1310720 | tf_op jit(solution)/shard_map/reduce_scatter | solution.py:31
Sparse Core Ops, SparseCore 0:
  10.7 47.1 all-gather.2
  60.8 50.5 all-gather.4
  243.1 46.4 reduce-scatter.2
  292.0 20.9 reduce-scatter.4
where the time goes:
time: 367 us; the launch traced here: 365 us
  waiting for transfers between devices  145 us (40%)
  matrix products  108 us (29%)
  blocking collectives  65 us (18%)
  local copies, waits for them, and re-layouts  22.7 us (6%)
  between operations  13.9 us (4%)
  other arithmetic  7.86 us (2%)
    dot_general x133, matrix products, product_high(): jnp.dot(first, second, precision=highest, preferred_element_type=jnp.floa...  108 us
    unnamed x1, blocking collectives  65 us
    all_gather x1, waiting for transfers between devices, on_device(): whole = lax.all_gather(whole_rows, 'col', axis=2, tiled=True)  50.3 us
    all_gather x1, waiting for transfers between devices, rows_first(): filled = lax.all_gather(both, axis, axis=0, tiled=True)  48.1 us
    reduce_scatter x2, waiting for transfers between devices, sum_by_axis(): nearer = lax.psum_scatter(value, axes[0], scatter_dimension=dim, tiled=True)  46.6 us
    unnamed x14, local copies, waits for them, and re-layouts  9.29 us
    dynamic_update_slice x16, local copies, waits for them, and re-layouts, advance(): solved = lax.dynamic_update_slice_in_dim(solved, value, start, 2)  7.65 us
  transfers between devices with their start and end apart: 4, of which 3 were waited for; matrix products, arithmetic and copies ran while one was open for 1% of the time, Pallas kernels for 0%

commit v1 on v0

--- a/solution.py
+++ b/solution.py
@@ -15,7 +15,9 @@
     turned = [jnp.moveaxis(a, dim, 0) for a, dim in zip(arrays, dims)]
     widths = [t[0].size for t in turned]
     both = jnp.concatenate([t.reshape(-1, w) for t, w in zip(turned, widths)], axis=1)
-    filled = lax.all_gather(both, axis, axis=0, tiled=True)
+    filled = jnp.concatenate(
+        lax.all_to_all(jnp.stack([both] * lax.axis_size(axis)), axis, 0, 0), axis=0
+    )
     pieces = jnp.split(filled, [sum(widths[:k]) for k in range(1, len(widths))], axis=1)
     return tuple(
         (

time: 367 us -> 351 us (0.956)
  waiting for transfers between devices: 145 us -> 96.3 us
  blocking collectives: 65 us -> 99.7 us
    all_gather x1 -> x0, waiting for transfers between devices: 48.1 us -> none  [rows_first(): filled = lax.all_gather(both, axis, axis=0, tiled=True)]
    all_to_all x0 -> x1, blocking collectives: none -> 34.7 us  [rows_first(): lax.all_to_all(jnp.stack([both] * lax.axis_size(axis)), axis, 0, 0)]
  transfers between devices with their start and end apart: 4 -> 3, of which waited for: 3 -> 2; matrix products, arithmetic and copies ran while one was open for 1% -> 1% of each run, Pallas kernels for 0% -> 0%
where the time goes in v1:
time: 351 us; the launch traced here: 349 us
  matrix products  108 us (31%)
  blocking collectives  99.7 us (28%)
  waiting for transfers between devices  96.3 us (27%)
  local copies, waits for them, and re-layouts  21.9 us (6%)
  between operations  13.9 us (4%)
  other arithmetic  7.2 us (2%)
    dot_general x133, matrix products, product_high(): jnp.dot(first, second, precision=highest, preferred_element_type=jnp.floa...  108 us
    unnamed x1, blocking collectives  64.9 us
    all_gather x1, waiting for transfers between devices, on_device(): whole = lax.all_gather(whole_rows, 'col', axis=2, tiled=True)  49.7 us
    reduce_scatter x2, waiting for transfers between devices, sum_by_axis(): nearer = lax.psum_scatter(value, axes[0], scatter_dimension=dim, tiled=True)  46.6 us
    all_to_all x1, blocking collectives, rows_first(): lax.all_to_all(jnp.stack([both] * lax.axis_size(axis)), axis, 0, 0)  34.7 us
    unnamed x14, local copies, waits for them, and re-layouts  9.3 us
    dynamic_update_slice x16, local copies, waits for them, and re-layouts, advance(): solved = lax.dynamic_update_slice_in_dim(solved, value, start, 2)  7.65 us
  transfers between devices with their start and end apart: 3, of which 2 were waited for; matrix products, arithmetic and copies ran while one was open for 1% of the time, Pallas kernels for 0%

profile of v1, /device:TPU:1, one launch (start us, length us, event | category | flops | bytes accessed | tf_op | source)
XLA Modules:
  0.0 349.0 jit_solution(11621978427025995279)
XLA Ops:
  9.4 34.7 %all_to_all.5 = f32[16,64,448]{2,1,0:T(8,128)S(1)} all-to-all(f32[16,64,448]{2,1,0:T(8,128)S(1)} %stack.70), channel_id=1, replica_groups=mesh['row_0'=4,'row_1'=4,'col'=8] {'row_0','row_1'}, dimensions={0} | all-to-all | bytes 3670016 | tf_op jit(solution)/shard_map/all_to_all | solution.py:19
  44.2 1.4 copy.31
  46.2 49.7 %all-gather.2.cloned.1.call-done = f32[2,1024,1024]{1,2,0:T(8,128)} async-done(((f32[2,1024,128]{1,2,0:T(8,128)}), f32[2,1024,1024]{1,2,0:T(8,128)}) %all-gather.2.cloned.1.call-update) | async-done | bytes 8388624 | tf_op jit(solution)/shard_map/all_gather | solution.py:76
  95.9 8.7 %copy.33 = f32[2,1024,1024]{2,1,0:T(8,128)} copy(f32[2,1024,1024]{1,2,0:T(8,128)} %all-gather.2.cloned.1.call-done) | data formatting | bytes 16777216
  104.6 106.3 %while.16 = (s32[]{:T(128)}, f32[2,32,1024]{2,1,0:T(8,128)S(1)}, f32[2,32,1024]{2,1,0:T(8,128)S(1)}, f32[2,32,1024]{2,1,0:T(8,128)S(1)}, f32[2,1024,64]{1,2,0:T(...) while((s32[]{:T(128)}, f32[2,32,1024]{2,1,0:T(8,128)S(1)}, ...), condition=%wide.region_1.0_spmd.clone, body=%wide.region_0.0_spmd.clone.sunk | while | flops 107294728 | bytes 3555570 | solution.py:64
  107.0 1.2 fusion.60
  113.5 1.2 fusion.60
  120.3 1.2 fusion.60
  133.6 1.2 fusion.60
  146.9 1.2 fusion.60
  153.4 1.2 fusion.60
  160.2 1.2 fusion.60
  173.5 1.2 fusion.60
  180.1 1.2 fusion.60
  186.8 1.2 fusion.60
  200.2 1.2 fusion.60
  210.9 4.0 %fusion.20 = f32[32,16384]{1,0:T(8,128)S(1)} fusion(f32[2,64,16384]{2,1,0:T(8,128)} %param.12, f32[2,32,1024]{2,1,0:T(8,128)S(1)} %get-tuple-element.112, s32[]{:T(128)S(6)} %select_n.23), kind=kOutput, calls=%fused_computation.37 | convolution fusion | flops 402653184 | bytes 6307844 | tf_op jit(solution)/shard_map/dot_general | solution.py:38
  215.0 4.1 %fusion.18 = f32[32,16384]{1,0:T(8,128)S(1)} fusion(f32[2,64,16384]{2,1,0:T(8,128)} %param.12, f32[2,32,1024]{2,1,0:T(8,128)S(1)} %get-tuple-element.112, s32[]{:T(128)S(6)} %add.84, s32[]{:T(128)S(6)} %select_n.23), kind=kOutput, calls=%fused_computation.35 | convolution fusion | flops 402653184 | bytes 6307848 | tf_op jit(solution)/shard_map/dot_general | solution.py:38
  219.1 3.9 %fusion.14 = f32[1,32,16384]{2,1,0:T(8,128)S(1)} fusion(f32[32,16384]{1,0:T(8,128)S(1)} %fusion.18, f32[2,64,16384]{2,1,0:T(8,128)} %param.12, f32[2,32,1024]{2,1,0:T(8,128)S(1)} %get-tuple-element.112, s32[]{:T(128)S(6)} %select_n.23), kind=kOutput, calls=%fused_computation.29 | convolution fusion | flops 403177472 | bytes 8404996 | tf_op jit(solution)/shard_map/dot_general | solution.py:38
  223.0 2.2 fusion.15
  225.2 2.2 pad_maximum_fusion.1
  227.5 46.6 %reduce-scatter.3.cloned.1.call-done = f32[2,32,4096]{2,1,0:T(8,128)} async-done(((f32[2,32,16384]{2,1,0:T(8,128)}), f32[2,32,4096]{2,1,0:T(8,128)}) %reduce-scatter.3.cloned.1.call-update) | async-done | bytes 1048592 | tf_op jit(solution)/shard_map/reduce_scatter | solution.py:33
  274.6 64.9 %all-reduce = f32[512]{0:T(512)S(1)} all-reduce(f32[512]{0:T(512)S(1)} %bitcast.137), channel_id=4, replica_groups=mesh['row_0'=4,'row_1'=4,'col'=8] {'row_0','row_1','col'}, use_global_device_ids=true, to_apply=%region_5.0.clone | all-reduce | flops 512 | bytes 4096
  340.8 1.7 sub.32
  (236 shorter events, 95.5 us)
Async XLA Ops:
  7.2 1.9 copy-start
  7.2 88.8 %all-gather.2.cloned.1.call-start = ((), (), s32[]{:S(2)}) async-start(), calls=%async_computation.3 | async-start | bytes 9437184 | tf_op jit(solution)/shard_map/all_gather | solution.py:76
  45.6 228.5 %reduce-scatter.3.cloned.1.call-start = ((), (), s32[]{:S(2)}) async-start(), calls=%async_computation.4 | async-start | bytes 5242880 | tf_op jit(solution)/shard_map/reduce_scatter | solution.py:33
  210.9 12.1 %slice-start = ((s8[8388608]{0:T(1024)(128)(4,1)}), s8[4194304]{0:T(1024)(128)(4,1)S(1)}, s32[]{:S(2)}) async-start(s8[8388608]{0:T(1024)(128)(4,1)} %bitcast.125), calls=%async_computation.6 | async-start | bytes 8388608
  215.0 8.0 %slice-start.1 = ((s8[8388608]{0:T(1024)(128)(4,1)}), s8[4194304]{0:T(1024)(128)(4,1)S(1)}, s32[]{:S(2)}) async-start(s8[8388608]{0:T(1024)(128)(4,1)} %bitcast.125), calls=%async_computation.7 | async-start | bytes 8388608
  227.5 46.7 %copy-start.3 = (s32[64]{0:T(128)S(1)}, s32[64]{0:T(128)}, u32[]{:S(2)}) copy-start(s32[64]{0:T(128)} %param.15) | copy-start | bytes 772
  227.5 46.8 %copy-start.2 = (f32[2,64]{1,0:T(2,128)S(1)}, f32[2,64]{1,0:T(2,128)}, u32[]{:S(2)}) copy-start(f32[2,64]{1,0:T(2,128)} %param.14) | copy-start | bytes 1540
  227.5 113.4 %copy-start.1 = (f32[2,32,1024]{2,1,0:T(8,128)S(1)}, f32[2,32,1024]{2,1,0:T(8,128)}, u32[]{:S(2)}) copy-start(f32[2,32,1024]{2,1,0:T(8,128)} %param.13) | copy-start | bytes 786436
  227.5 113.3 %reduce-scatter.5.cloned.1.call-start = ((), (), s32[]{:S(2)}) async-start(), calls=%async_computation.5 | async-start | bytes 1310720 | tf_op jit(solution)/shard_map/reduce_scatter | solution.py:33
Sparse Core Ops, SparseCore 0:
  45.7 50.1 all-gather.1
  227.6 46.4 reduce-scatter.2
  276.6 21.9 reduce-scatter.4
